TPU v7x, 512 devices: a whole 4x4x16 slice. The times are simulated.
512 devices in a mesh: tok: 32 (over z, core), par: 16 (over x, y).
Axes of the slice: x: 4, y: 4, z: 16, core: 2. Of those that a mesh axis runs over, the one named last changes fastest.
Arguments:
- query_grads: bfloat16 [4, 8192, 28672], P(None, 'tok', 'par'), as said below
- start_block: bfloat16 [28672, 128], P('par', 'tok'), may hold values from -6 to 6
- hooked_out: bfloat16 [8192, 8192], P('tok', 'par'), may hold values from -6 to 6
- hooked_in: bfloat16 [8192, 28672], P('tok', 'par'), may hold values from -6 to 6
Outputs:
- scores: float32 [4, 8192], P(None, 'tok')
Inputs may be any that keep to these rules, and one draw needn't show every extreme that they name: `query_grads`: Real-valued gradient matrices, of full rank.
All inputs are finite; a program needn't handle non-finite values.
Results may differ from a plain program's by a relative error of at most 0.006.
Values may be sent and summed in bfloat16 or wider, within the bound.
A program may use at most 64 MiB of HBM per device.

v0:
```python
import jax
import jax.numpy as jnp
from jax import lax
from jax.sharding import PartitionSpec as P

RANK = 32
ITERS = 2


def local_gram(images):
    blocks = images.reshape(images.shape[0], images.shape[1] // RANK, RANK)
    return jnp.einsum("oqr,oqs->qrs", blocks, blocks, precision=lax.Precision.HIGHEST)


def from_gram(images, gram_sum):
    blocks = images.reshape(images.shape[0], images.shape[1] // RANK, RANK)
    chol_factor = jnp.linalg.cholesky(gram_sum)
    solved = lax.linalg.triangular_solve(
        chol_factor, jnp.transpose(blocks, (1, 2, 0)), left_side=True, lower=True
    )
    return jnp.transpose(solved, (2, 0, 1)).reshape(images.shape).astype(jnp.bfloat16)


def on_device(query_grads, start_block, hooked_out, hooked_in):
    queries = query_grads.shape[0]
    rows_tok = query_grads.shape[1]
    cols_par = hooked_out.shape[1]
    subspace = lax.all_gather(start_block, "tok", axis=1, tiled=True)
    local_basis = None
    for iteration in range(ITERS):
        sub_blocks = subspace.reshape(subspace.shape[0], queries, RANK)
        partial_value = jnp.einsum(
            "qoi,iqr->oqr", query_grads, sub_blocks, preferred_element_type=jnp.float32
        )
        images = lax.psum(partial_value.reshape(rows_tok, queries * RANK), "par")
        gram_sum = lax.psum(local_gram(images), "tok")
        local_basis = from_gram(images, gram_sum)
        basis_blocks = local_basis.reshape(rows_tok, queries, RANK)
        back_terms = jnp.einsum(
            "qoi,oqr->iqr", query_grads, basis_blocks, preferred_element_type=jnp.float32
        )
        summed = lax.psum(back_terms.reshape(back_terms.shape[0], queries * RANK), "tok")
        subspace = summed.astype(jnp.bfloat16)
    gathered = lax.all_gather(local_basis, "tok", axis=0, tiled=True)
    basis_par = lax.dynamic_slice_in_dim(gathered, lax.axis_index("par") * cols_par, cols_par, 0)
    out_proj = jnp.dot(hooked_out, basis_par, preferred_element_type=jnp.float32)
    in_proj = jnp.dot(hooked_in, subspace, preferred_element_type=jnp.float32)
    whole_out, whole_in = lax.psum((out_proj, in_proj), "par")
    token_scores = (whole_out * whole_in).reshape(whole_out.shape[0], queries, RANK).sum(axis=2)
    return token_scores.T


def solution(mesh):
    placed = (P(None, "tok", "par"), P("par", "tok"), P("tok", "par"), P("tok", "par"))
    return jax.shard_map(
        on_device, mesh=mesh, in_specs=placed, out_specs=P(None, "tok"), check_vma=False
    )
```

profile of v0, /device:TPU:1, one launch (start us, length us, event | category | flops | bytes accessed | tf_op | source)
XLA Modules:
  0.0 835.8 jit_solution(13217683122498133509)
XLA Ops:
  6.5 0.0 copy-start
  6.5 0.0 all-reduce.7.cloned.1.call-start
  6.5 39.2 %all-gather = bf16[32,4,1792]{2,1,0:T(4,128)(2,1)S(1)} all-gather(bf16[1,4,1792]{2,1,0:T(4,128)(2,1)} %bitcast.74), channel_id=1, replica_groups=mesh['tok'=32,'par'=16] {'tok'}, dimensions={0}, use_global_device_ids=true | all-gather | bytes 473088 | tf_op jit(solution)/shard_map/all_gather | solution.py:28
  45.7 0.1 reshape.60
  45.8 3.9 convolution_bitcast_fusion.3
  49.7 0.0 all-reduce.7.cloned.1.call-update
  49.7 0.0 all-reduce.9.cloned.1.call-start
  49.8 107.0 %all-reduce.7.cloned.1.call-done = f32[256,4,32]{0,2,1:T(8,128)} async-done(((f32[256,4,32]{0,2,1:T(8,128)}), f32[256,4,32]{0,2,1:T(8,128)}) %all-reduce.7.cloned.1.call-update) | async-done | bytes 131088 | tf_op jit(solution)/shard_map/psum | solution.py:35
  156.8 1.2 fusion.12
  158.1 90.6 %psum.57 = f32[4,32,32]{1,2,0:T(8,128)S(1)} all-reduce(f32[4,32,32]{1,2,0:T(8,128)S(1)} %fusion.12), channel_id=1, replica_groups=mesh['tok'=32,'par'=16] {'tok'}, use_global_device_ids=true, to_apply=%region_1.0 | all-reduce | flops 4096 | bytes 32768 | tf_op jit(solution)/shard_map/psum | solution.py:36
  248.7 0.1 copy.16
  248.8 11.7 %custom-call.8 = f32[4,32,32]{2,1,0:T(8,128)S(1)} custom-call(f32[4,32,32]{2,1,0:T(8,128)S(1)} %fusion.10), custom_call_target="Cholesky" | custom-call | tf_op jit(solution)/shard_map/jit(cholesky)/cholesky | solution.py:17
  260.5 0.1 compare_reduce_fusion.1
  260.7 0.1 select_bitcast_fusion.1
  260.7 9.8 %custom-call.9 = f32[4,1,32,32]{2,3,1,0:T(8,128)S(1)} custom-call(f32[4,1,32,32]{3,2,1,0:T(8,128)S(1)} %select_bitcast_fusion.1), custom_call_target="InvertDiagBlocksLowerTriangular" | custom-call | tf_op jit(solution)/shard_map/triangular_solve/custom-call.0 | solution.py:18
  270.6 1.2 fusion
  271.8 2.8 fusion.13
  274.6 98.8 %all-reduce.12 = bf16[1792,128]{0,1:T(8,128)(2,1)S(1)} all-reduce(f32[1792,128]{0,1:T(8,128)S(1)} %bitcast.69), channel_id=1, replica_groups=mesh['tok'=32,'par'=16] {'tok'}, use_global_device_ids=true, to_apply=%region_4.7 | all-reduce | flops 229376 | bytes 1376256 | tf_op jit(solution)/shard_map/psum | solution.py:42
  373.4 3.9 convolution_bitcast_fusion.2
  377.3 0.0 all-reduce.9.cloned.1.call-update
  377.3 0.0 all-gather.3.cloned.1.call-start
  377.3 112.2 %all-reduce.9.cloned.1.call-done = f32[256,4,32]{0,2,1:T(8,128)} async-done(((f32[256,4,32]{0,2,1:T(8,128)}), f32[256,4,32]{0,2,1:T(8,128)}) %all-reduce.9.cloned.1.call-update) | async-done | bytes 131088 | tf_op jit(solution)/shard_map/psum | solution.py:35
  489.5 1.2 fusion.14
  490.7 90.6 %psum.60 = f32[4,32,32]{1,2,0:T(8,128)S(1)} all-reduce(f32[4,32,32]{1,2,0:T(8,128)S(1)} %fusion.14), channel_id=1, replica_groups=mesh['tok'=32,'par'=16] {'tok'}, use_global_device_ids=true, to_apply=%region_6.9 | all-reduce | flops 4096 | bytes 32768 | tf_op jit(solution)/shard_map/psum | solution.py:36
  581.3 0.1 copy.19
  581.4 11.7 %custom-call.10 = f32[4,32,32]{2,1,0:T(8,128)S(1)} custom-call(f32[4,32,32]{2,1,0:T(8,128)S(1)} %fusion.8), custom_call_target="Cholesky" | custom-call | tf_op jit(solution)/shard_map/jit(cholesky)/cholesky | solution.py:17
  593.2 0.1 compare_reduce_fusion
  593.3 0.1 select_bitcast_fusion
  593.4 9.8 %custom-call.11 = f32[4,1,32,32]{2,3,1,0:T(8,128)S(1)} custom-call(f32[4,1,32,32]{3,2,1,0:T(8,128)S(1)} %select_bitcast_fusion), custom_call_target="InvertDiagBlocksLowerTriangular" | custom-call | tf_op jit(solution)/shard_map/triangular_solve/custom-call.0 | solution.py:18
  603.2 1.9 convolution_convert_fusion
  605.1 0.0 all-gather.3.cloned.1.call-update
  605.1 0.0 all-reduce.11.cloned.1.call-start
  605.2 0.0 copy-start.1
  605.2 2.8 fusion.5
  608.0 100.7 %all-reduce.13 = bf16[1792,128]{0,1:T(8,128)(2,1)S(1)} all-reduce(f32[1792,128]{0,1:T(8,128)S(1)} %bitcast.70), channel_id=1, replica_groups=mesh['tok'=32,'par'=16] {'tok'}, use_global_device_ids=true, to_apply=%region_8.11 | all-reduce | flops 229376 | bytes 1376256 | tf_op jit(solution)/shard_map/psum | solution.py:42
  708.7 0.0 copy-done
  708.7 1.1 convolution_bitcast_fusion.1
  709.8 0.0 all-gather.3.cloned.1.call-done
  709.8 0.0 copy-done.1
  709.8 1.8 convolution_bitcast_fusion
  711.6 0.0 all-reduce.11.cloned.1.call-update
  711.6 116.0 %all-reduce.11.cloned.1.call-done = (f32[256,128]{0,1:T(8,128)}, f32[256,128]{0,1:T(8,128)}) async-done(((f32[256,128]{0,1:T(8,128)}, f32[256,128]{0,1:T(8,128)}), (f32[256,128]{0,1:T(8,128)}, f32[256,128]{0,1:T(8,128)})) %all-reduce.11.cloned.1.call-update) | async-done | bytes 262160 | tf_op jit(solution)/shard_map/psum | solution.py:48
  827.7 1.6 bitcast_reduce_fusion
  (6 shorter events, 0.1 us)
Async XLA Ops:
  6.5 702.2 %copy-start = (bf16[256,1792]{1,0:T(8,128)(2,1)S(1)}, bf16[256,1792]{1,0:T(8,128)(2,1)}, u32[]{:S(2)}) copy-start(bf16[256,1792]{1,0:T(8,128)(2,1)} %param.10) | copy-start | bytes 2752516
  6.5 150.3 %all-reduce.7.cloned.1.call-start = ((), (), s32[]{:S(2)}) async-start(), calls=%async_computation | async-start | bytes 262144 | tf_op jit(solution)/shard_map/psum | solution.py:35
  49.7 439.8 %all-reduce.9.cloned.1.call-start = ((), (), s32[]{:S(2)}) async-start(), calls=%async_computation.1 | async-start | bytes 262144 | tf_op jit(solution)/shard_map/psum | solution.py:35
  377.3 332.6 %all-gather.3.cloned.1.call-start = ((), (), s32[]{:S(2)}) async-start(), calls=%async_computation.2 | async-start | bytes 2162688 | tf_op jit(solution)/shard_map/all_gather | solution.py:44
  605.1 222.5 %all-reduce.11.cloned.1.call-start = ((), (), s32[]{:S(2)}) async-start(), calls=%async_computation.3 | async-start | bytes 524288 | tf_op jit(solution)/shard_map/psum | solution.py:48
  605.2 104.7 %copy-start.1 = (bf16[256,512]{1,0:T(8,128)(2,1)S(1)}, bf16[256,512]{1,0:T(8,128)(2,1)}, u32[]{:S(2)}) copy-start(bf16[256,512]{1,0:T(8,128)(2,1)} %param.9) | copy-start | bytes 786436
Sparse Core Ops, SparseCore 0:
  49.8 106.9 all-reduce.6
  377.4 112.0 all-reduce.8
  605.2 75.7 all-gather.2
  711.8 115.8 all-reduce.10
where the time goes:
time: 836 us
  blocking collectives  420 us (50%)
  waiting for transfers between devices  335 us (40%)
  other arithmetic  45.2 us (5%)
  matrix products  21.8 us (3%)
  between operations  13.2 us (2%)
    psum x2, waiting for transfers between devices, on_device(): images = lax.psum(partial_value.reshape(rows_tok, queries * RANK), 'par')  219 us
    psum x2, blocking collectives, on_device(): lax.psum(back_terms.reshape(back_terms.shape[0], queries * RANK), 'tok')  199 us
    psum x2, blocking collectives, on_device(): gram_sum = lax.psum(local_gram(images), 'tok')  181 us
    psum x1, waiting for transfers between devices, on_device(): whole_out, whole_in = lax.psum((out_proj, in_proj), 'par')  116 us
    all_gather x1, blocking collectives, on_device(): subspace = lax.all_gather(start_block, 'tok', axis=1, tiled=True)  39.2 us
    another operation x7, other arithmetic, from_gram(): chol_factor = jnp.linalg.cholesky(gram_sum)  23.8 us
    another operation x5, other arithmetic, from_gram(): lax.linalg.triangular_solve(chol_factor, jnp.transpose(blocks, (1, 2, 0))...  19.9 us
  transfers between devices with their start and end apart: 4, of which 3 were waited for; matrix products, arithmetic and copies ran while one was open for 0% of the time, Pallas kernels for 0%

commit v1 on v0

v1 whole, which is shorter than its diff:
```python
import types

import jax
import jax.numpy as jnp
from jax import lax
from jax.experimental import pallas as pl
from jax.experimental.pallas import tpu as pltpu
from jax.sharding import PartitionSpec as P

MESH = pl.DeviceIdType.MESH
F32, BF16 = jnp.float32, jnp.bfloat16
HIGH = lax.Precision.HIGHEST
RANK = 32
ITERS = 2
QUERIES = 4
COLS = QUERIES * RANK
LANES = 128
Z = 16
PAR = 16
ROWS = 256
FEATS = 1792
TILES = FEATS // LANES
OUTS = 512
PIECE = 512
PIECES = 4
CHUNK = ROWS // PAR
HALF = COLS // 2

TREE = {0: (1, -1), 3: (1, -1), -3: (1, -1), 6: (1, -1, 2), -6: (1, -1)}
RELAYS = (6, -6, 3, -3)
ARRIVALS = (3, -3, 6, -6)
LEAVES = [(r, f) for r in (6, -6, 3, -3, 0) for f in TREE[r]]
ORDER = (10, 6, 9, 7, 11, 5, 2, 14, 8, 13, 3, 15, 1, 12, 4)


def nt(a, b, precision=None):
    return lax.dot_general(
        a, b, (((1,), (1,)), ((), ())), precision=precision, preferred_element_type=F32
    )


def remote(src, dst, send_sem, recv_sem, device):
    return pltpu.make_async_remote_copy(
        src_ref=src, dst_ref=dst, send_sem=send_sem, recv_sem=recv_sem,
        device_id=device, device_id_type=MESH,
    )


def drain(ref, sem):
    pltpu.make_async_copy(ref, ref, sem).wait()


def inverse_factor(gram):
    lane = lax.broadcasted_iota(jnp.int32, (RANK, COLS), 1)
    row = lax.broadcasted_iota(jnp.int32, (RANK, COLS), 0)
    first = lane - lane % RANK
    columns = [
        jnp.take_along_axis(gram, first + j, axis=1, mode="promise_in_bounds") for j in range(RANK)
    ]
    w = jnp.where(lane - first == row, 1.0, 0.0).astype(F32)
    for j in range(RANK):
        pivot = columns[j][j : j + 1, :]
        scale = lax.rsqrt(pivot)
        scale = scale * (1.5 - 0.5 * pivot * scale * scale)
        u = columns[j] * scale
        for k in range(j + 1, RANK):
            columns[k] = columns[k] - u * u[k : k + 1, :]
        row_w = w[j : j + 1, :] * scale
        w = jnp.where(row == j, row_w, jnp.where(row > j, w - u * row_w, w))
    return w


def block_diagonal(w):
    rows = lax.broadcasted_iota(jnp.int32, (COLS, COLS), 0)
    lanes = lax.broadcasted_iota(jnp.int32, (COLS, COLS), 1)
    return jnp.where(rows // RANK == lanes // RANK, jnp.concatenate([w] * QUERIES, axis=0), 0.0)


def kernel(names, *refs):
    m = types.SimpleNamespace(**dict(zip(names, refs)))
    tok, par = lax.axis_index("tok"), lax.axis_index("par")
    z, core = tok // 2, tok % 2

    def chip(offset):
        return (lax.rem(tok + 2 * offset + 2 * Z, 2 * Z), par)

    def at_z(offset):
        return lax.rem(z + offset + Z, Z)

    def peer(k):
        return lax.rem(par + k, PAR)

    sent = []
    sibling = (tok + 1 - 2 * core, par)

    loads = [
        pltpu.make_async_copy(m.grads.at[q], m.g.at[q], m.load_sem.at[q])
        for q in range(QUERIES)
    ] + [
        pltpu.make_async_copy(m.hook_out, m.ho, m.load_sem.at[QUERIES]),
        pltpu.make_async_copy(m.hook_in, m.hi, m.load_sem.at[QUERIES + 1]),
    ]
    barrier = pltpu.get_barrier_semaphore()
    for k in range(1, Z):
        pl.semaphore_signal(barrier, inc=1, device_id=chip(k), device_id_type=MESH)
    pl.semaphore_signal(barrier, inc=1, device_id=sibling, device_id_type=MESH)
    for k in range(1, PAR):
        pl.semaphore_signal(barrier, inc=1, device_id=(tok, peer(k)), device_id_type=MESH)

    for load in loads:
        load.start()

    start = m.start[...].astype(F32)
    tail = jnp.concatenate(
        [start[:, 3 * PIECE :], jnp.zeros((start.shape[0], PIECES * PIECE - FEATS), F32)], axis=1
    )
    pieces = [start[:, k * PIECE : (k + 1) * PIECE] for k in range(PIECES - 1)] + [tail]
    m.s0[core, z] = jnp.concatenate(pieces, axis=0).astype(BF16)
    for it in range(ITERS):
        for k in range(TILES, Z):
            m.part[it, k] = jnp.zeros((HALF, LANES), F32)

    pl.semaphore_wait(barrier, Z - 1 + 1 + PAR - 1)

    def z_gather(buf, send_sem, recv_sem):
        own = buf.at[z]
        for r in RELAYS + TREE[0]:
            remote(own, own, send_sem, recv_sem.at[r % Z], chip(r)).start()
        for r in ARRIVALS:
            block = buf.at[at_z(-r)]
            drain(block, recv_sem.at[r % Z])
            for f in TREE[r]:
                remote(block, block, send_sem, recv_sem.at[(r + f) % Z], chip(f)).start()
        relayed = [r % Z for r in RELAYS]
        for k in range(1, Z):
            if k not in relayed:
                drain(buf.at[at_z(-k)], recv_sem.at[k])
        sent.append((buf.at[pl.ds(0, Z - 1)], send_sem))

    def par_scatter(src, dst, send_sem, recv_sem):
        for k in ORDER:
            remote(src.at[peer(k)], dst.at[k - 1], send_sem, recv_sem, (tok, peer(k))).start()
        sent.append((dst, send_sem))

    def par_gather(buf, send_sem, recv_sem):
        own = buf.at[par]
        for k in ORDER:
            remote(own, own, send_sem, recv_sem, (tok, peer(k))).start()
        sent.append((buf.at[pl.ds(0, PAR - 1)], send_sem))

    def swap(buf, send_sem, recv_sem):
        remote(buf.at[core], buf.at[core], send_sem, recv_sem, sibling).start()
        sent.append((buf.at[core], send_sem))

    z_gather(m.s0.at[core], m.s0_ss.at[0], m.s0_rs)
    swap(m.s0, m.s0_ss.at[1], m.s0_rs.at[0])
    for q in range(QUERIES):
        loads[q].wait()
    drain(m.s0.at[1 - core], m.s0_rs.at[0])
    even, odd = m.s0[0].astype(F32), m.s0[1].astype(F32)
    for k in range(PIECES):
        rows = slice(k * 4, k * 4 + 4)
        both = jnp.concatenate([even[:, rows, :], odd[:, rows, :]], axis=1)
        m.s0t[:, k * PIECE : (k + 1) * PIECE] = both.reshape(COLS, PIECE).astype(BF16)
    images = jnp.concatenate(
        [nt(m.g[q], m.s0t[q * RANK : (q + 1) * RANK, :FEATS]) for q in range(QUERIES)], axis=1
    )

    def tiles_of(buf, plane, first):
        return jnp.concatenate(
            [buf[plane, k, first : first + RANK, :] for k in range(TILES)], axis=1
        )

    for it in range(ITERS):
        m.img[it] = images.reshape(PAR, CHUNK, COLS)
        par_scatter(m.img.at[it], m.img_in.at[it], m.img_ss.at[it], m.img_rs.at[it])
        drain(m.img_in.at[it], m.img_rs.at[it])
        m.whole[it, par] = m.img[it, par] + jnp.sum(m.img_in[it], axis=0)
        par_gather(m.whole.at[it], m.whole_ss.at[it], m.whole_rs.at[it])
        drain(m.whole.at[it, pl.ds(0, PAR - 1)], m.whole_rs.at[it])

        if it == ITERS - 1:
            @pl.when(z == par)
            def _():
                for k in range(1, Z):
                    remote(
                        m.whole.at[it, at_z(k)], m.brow, m.brow_ss, m.brow_rs, chip(k)
                    ).start()
                m.brow_own[...] = m.whole[it, z]

        turned = m.whole[it].reshape(ROWS, COLS).T
        gram = nt(turned, turned, HIGH)
        lane = lax.broadcasted_iota(jnp.int32, (RANK, COLS), 1)
        packed = jnp.zeros((RANK, COLS), F32)
        for q in range(QUERIES):
            packed = jnp.where(lane // RANK == q, gram[q * RANK : (q + 1) * RANK, :], packed)
        m.gram_out[it] = packed
        remote(
            m.gram_out.at[it], m.gram_in.at[it],
            m.gram_ss.at[it, 0], m.gram_rs.at[it, 0], sibling,
        ).start()
        sent.append((m.gram_out.at[it], m.gram_ss.at[it, 0]))

        high = turned.astype(BF16)
        low = (turned - high.astype(F32)).astype(BF16)
        for q in range(QUERIES):
            cut = slice(q * RANK, (q + 1) * RANK)
            m.split[q] = jnp.concatenate([high[cut], low[cut]], axis=0)

        def back(q):
            both = jnp.dot(m.split[q], m.g[q], preferred_element_type=F32)
            return both[:RANK] + both[RANK:]

        for i in range(2):
            terms = back(2 * (1 - core) + i)
            for k in range(TILES):
                m.give[it, i, k] = terms[:, k * LANES : (k + 1) * LANES]
            remote(
                m.give.at[it, i], m.take.at[it, i],
                m.give_ss.at[it, i], m.take_rs.at[it, i], sibling,
            ).start()
            sent.append((m.give.at[it, i], m.give_ss.at[it, i]))

        drain(m.gram_in.at[it], m.gram_rs.at[it, 0])
        m.gram_rows[it] = (packed + m.gram_in[it]).reshape(PAR, 2, COLS)
        mine = m.gram_rows.at[it, par]
        for k in range(1, Z):
            remote(
                mine, m.gram_z.at[it, k - 1], m.gram_ss.at[it, 1], m.gram_rs.at[it, 1], chip(k)
            ).start()
        sent.append((m.gram_z.at[it], m.gram_ss.at[it, 1]))

        for i in range(2):
            terms = back(2 * core + i)
            drain(m.take.at[it, i], m.take_rs.at[it, i])
            for k in range(TILES):
                both = terms[:, k * LANES : (k + 1) * LANES] + m.take[it, i, k]
                m.part[it, k, i * RANK : (i + 1) * RANK, :] = both

        part = m.part.at[it]
        for slot, (r, f) in enumerate(LEAVES):
            remote(
                part.at[at_z(-r - f)], m.leaf.at[it, slot],
                m.leaf_ss.at[it], m.leaf_rs.at[it, slot], chip(-f),
            ).start()
        sent.append((m.leaf.at[it], m.leaf_ss.at[it]))

        drain(m.gram_z.at[it], m.gram_rs.at[it, 1])
        m.gram_all[it, par] = m.gram_rows[it, par] + jnp.sum(m.gram_z[it], axis=0)
        par_gather(m.gram_all.at[it], m.gram_ss.at[it, 2], m.gram_rs.at[it, 2])

        for n, r in enumerate(RELAYS):
            total = m.part[it, at_z(-r)]
            for slot, (rr, f) in enumerate(LEAVES):
                if rr == r:
                    drain(m.leaf.at[it, slot], m.leaf_rs.at[it, slot])
                    total = total + m.leaf[it, slot]
            m.relay[it, n] = total.astype(BF16)
            remote(
                m.relay.at[it, n], m.final.at[it, n],
                m.relay_ss.at[it], m.final_rs.at[it, n], chip(-r),
            ).start()
        sent.append((m.relay.at[it], m.relay_ss.at[it]))

        drain(m.gram_all.at[it, pl.ds(0, PAR - 1)], m.gram_rs.at[it, 2])
        full = m.gram_all[it].reshape(RANK, COLS)
        inverse = block_diagonal(inverse_factor(full))
        inverse_mine = jnp.where(
            core == 0, inverse[:HALF, :HALF], inverse[HALF:, HALF:]
        )

        total = m.part[it, z]
        for slot, (r, f) in enumerate(LEAVES):
            if r == 0:
                drain(m.leaf.at[it, slot], m.leaf_rs.at[it, slot])
                total = total + m.leaf[it, slot]
        for n in range(len(RELAYS)):
            drain(m.final.at[it, n], m.final_rs.at[it, n])
            total = total + m.final[it, n].astype(F32)
        turned_back = jnp.dot(inverse_mine, total, precision=HIGH, preferred_element_type=F32)
        sub = m.sub if it < ITERS - 1 else m.last
        sub[core, z, :HALF, :] = turned_back.astype(BF16)
        if it == ITERS - 1:
            @pl.when(z != par)
            def _():
                drain(m.brow, m.brow_rs)
                m.brow_own[...] = m.brow[...]
            sub[core, z, HALF:, :] = nt(m.brow_own[...], inverse, HIGH).astype(BF16)

        z_gather(sub.at[core], m.sub_ss.at[it, 0], m.sub_rs.at[it])
        swap(sub, m.sub_ss.at[it, 1], m.sub_rs.at[it, 0])
        if it < ITERS - 1:
            def pair(plane):
                return jnp.concatenate(
                    [nt(m.g[2 * plane + i], tiles_of(sub, plane, i * RANK)) for i in range(2)], axis=1
                )

            ours = pair(core)
            drain(sub.at[1 - core], m.sub_rs.at[it, 0])
            theirs = pair(1 - core)
            images = jnp.where(
                core == 0,
                jnp.concatenate([ours, theirs], axis=1),
                jnp.concatenate([theirs, ours], axis=1),
            )
        else:
            drain(sub.at[1 - core], m.sub_rs.at[it, 0])

    loads[QUERIES].wait()
    loads[QUERIES + 1].wait()
    last = m.last
    basis = jnp.concatenate(
        [last[plane, :, HALF:, :].reshape(ROWS, COLS) for plane in range(2)], axis=0
    )
    out_proj = jnp.dot(m.ho[...], basis, preferred_element_type=F32)
    subspace = jnp.concatenate(
        [tiles_of(last, q // 2, (q % 2) * RANK) for q in range(QUERIES)], axis=0
    )
    in_proj = nt(m.hi[...], subspace)
    m.proj[:, :CHUNK, :] = out_proj.reshape(PAR, CHUNK, COLS)
    m.proj[:, CHUNK:, :] = in_proj.reshape(PAR, CHUNK, COLS)
    par_scatter(m.proj, m.proj_in, m.proj_ss, m.proj_rs)
    lane8 = lax.broadcasted_iota(jnp.int32, (8, COLS), 1)
    row8 = lax.broadcasted_iota(jnp.int32, (8, COLS), 0)
    pick = jnp.where(lane8 // RANK == row8, 1.0, 0.0).astype(F32)
    m.placed[...] = jnp.zeros((LANES, COLS), F32)
    drain(m.proj_in, m.proj_rs)
    total = m.proj[par] + jnp.sum(m.proj_in[...], axis=0)
    m.placed[pl.ds(pl.multiple_of((par % 8) * CHUNK, CHUNK), CHUNK), :] = (
        total[:CHUNK] * total[CHUNK:]
    )
    m.score[par] = nt(pick, m.placed[...], HIGH)
    par_gather(m.score, m.score_ss, m.score_rs)
    drain(m.score.at[pl.ds(0, PAR - 1)], m.score_rs)
    for h in range(2):
        m.out[:, h * LANES : (h + 1) * LANES] = jnp.sum(
            m.score[h * 8 : h * 8 + 8], axis=0
        )[:QUERIES]

    for ref, sem in sent:
        drain(ref, sem)

    @pl.when(z == par)
    def _():
        drain(m.whole.at[ITERS - 1, pl.ds(0, Z - 1)], m.brow_ss)


def on_device(query_grads, start_block, hooked_out, hooked_in):
    vmem, dma = pltpu.VMEM, pltpu.SemaphoreType.DMA
    scratch = dict(
        g=vmem((QUERIES, ROWS, FEATS), BF16),
        ho=vmem((ROWS, OUTS), BF16),
        hi=vmem((ROWS, FEATS), BF16),
        load_sem=dma((QUERIES + 2,)),
        s0=vmem((2, Z, 4 * PIECES, PIECE), BF16),
        s0_ss=dma((2,)),
        s0_rs=dma((Z,)),
        s0t=vmem((COLS, PIECES * PIECE), BF16),
        img=vmem((ITERS, PAR, CHUNK, COLS), F32),
        img_in=vmem((ITERS, PAR - 1, CHUNK, COLS), F32),
        img_ss=dma((ITERS,)),
        img_rs=dma((ITERS,)),
        whole=vmem((ITERS, PAR, CHUNK, COLS), F32),
        whole_ss=dma((ITERS,)),
        whole_rs=dma((ITERS,)),
        brow=vmem((CHUNK, COLS), F32),
        brow_own=vmem((CHUNK, COLS), F32),
        brow_ss=dma,
        brow_rs=dma,
        gram_out=vmem((ITERS, RANK, COLS), F32),
        gram_in=vmem((ITERS, RANK, COLS), F32),
        gram_rows=vmem((ITERS, PAR, 2, COLS), F32),
        gram_z=vmem((ITERS, Z - 1, 2, COLS), F32),
        gram_all=vmem((ITERS, PAR, 2, COLS), F32),
        gram_ss=dma((ITERS, 3)),
        gram_rs=dma((ITERS, 3)),
        split=vmem((QUERIES, 2 * RANK, ROWS), BF16),
        give=vmem((ITERS, 2, TILES, RANK, LANES), F32),
        take=vmem((ITERS, 2, TILES, RANK, LANES), F32),
        give_ss=dma((ITERS, 2)),
        take_rs=dma((ITERS, 2)),
        part=vmem((ITERS, Z, HALF, LANES), F32),
        leaf=vmem((ITERS, len(LEAVES), HALF, LANES), F32),
        leaf_ss=dma((ITERS,)),
        leaf_rs=dma((ITERS, len(LEAVES))),
        relay=vmem((ITERS, len(RELAYS), HALF, LANES), BF16),
        final=vmem((ITERS, len(RELAYS), HALF, LANES), BF16),
        relay_ss=dma((ITERS,)),
        final_rs=dma((ITERS, len(RELAYS))),
        sub=vmem((2, Z, HALF, LANES), BF16),
        last=vmem((2, Z, HALF + CHUNK, LANES), BF16),
        sub_ss=dma((ITERS, 2)),
        sub_rs=dma((ITERS, Z)),
        proj=vmem((PAR, 2 * CHUNK, COLS), F32),
        proj_in=vmem((PAR - 1, 2 * CHUNK, COLS), F32),
        proj_ss=dma,
        proj_rs=dma,
        placed=vmem((LANES, COLS), F32),
        score=vmem((PAR, 8, LANES), F32),
        score_ss=dma,
        score_rs=dma,
    )
    names = ["grads", "start", "hook_out", "hook_in", "out"] + list(scratch)
    hbm = pl.BlockSpec(memory_space=pltpu.HBM)
    near = pl.BlockSpec(memory_space=pltpu.VMEM)

    def body(*refs):
        kernel(names, *refs)

    return pl.pallas_call(
        body,
        name="influence",
        out_shape=jax.ShapeDtypeStruct((QUERIES, ROWS), F32),
        in_specs=[hbm, near, hbm, hbm],
        out_specs=near,
        scratch_shapes=list(scratch.values()),
        compiler_params=pltpu.CompilerParams(
            collective_id=0, has_side_effects=True, vmem_limit_bytes=60 * 1024 * 1024
        ),
        cost_estimate=pl.CostEstimate(
            flops=8 * QUERIES * ROWS * FEATS * RANK, bytes_accessed=5_000_000, transcendentals=0
        ),
    )(query_grads, start_block.T, hooked_out, hooked_in)


def solution(mesh):
    placed = (P(None, "tok", "par"), P("par", "tok"), P("tok", "par"), P("tok", "par"))
    return jax.shard_map(
        on_device, mesh=mesh, in_specs=placed, out_specs=P(None, "tok"), check_vma=False
    )
```

time: 836 us -> 120 us (0.14)
  blocking collectives: 420 us -> 0 us
  waiting for transfers between devices: 335 us -> 0 us
  Pallas kernels: 0 us -> 119 us
  other arithmetic: 45.2 us -> 0 us
  matrix products: 21.8 us -> 0 us
  between operations: 13.2 us -> 0.01 us
    psum x4 -> x0, blocking collectives: 381 us -> none  [the longest x2 199 us: on_device(): lax.psum(back_terms.reshape(back_terms.shape[0], queries * RANK), 'tok')]
    psum x3 -> x0, waiting for transfers between devices: 335 us -> none  [the longest x2 219 us: on_device(): images = lax.psum(partial_value.reshape(rows_tok, queries * RANK), 'par')]
    pallas_call x0 -> x1, Pallas kernels: none -> 119 us  [on_device(): pl.pallas_call(body, name='influence', out_shape=jax.ShapeDtypeStruct((QU...]
    another operation x12 -> x0, other arithmetic: 43.6 us -> none  [the longest x7 23.8 us: from_gram(): chol_factor = jnp.linalg.cholesky(gram_sum)]
    all_gather x1 -> x0, blocking collectives: 39.2 us -> none  [on_device(): subspace = lax.all_gather(start_block, 'tok', axis=1, tiled=True)]
    dot_general x8 -> x0, matrix products: 18.7 us -> none  [the longest x2 7.73 us: on_device(): jnp.einsum('qoi,iqr->oqr', query_grads, sub_blocks, preferred_element_typ...]
  transfers between devices with their start and end apart: 4 -> 0, of which waited for: 3 -> 0; matrix products, arithmetic and copies ran while one was open for 0% -> 0% of each run, Pallas kernels for 0% -> 0%
where the time goes in v1:
time: 120 us
  Pallas kernels  119 us (99%)
  local copies, waits for them, and re-layouts  1.28 us (1%)
    pallas_call x1, Pallas kernels, on_device(): pl.pallas_call(body, name='influence', out_shape=jax.ShapeDtypeStruct((QU...  119 us

profile of v1, /device:TPU:1, one launch (start us, length us, event | category | flops | bytes accessed | tf_op | source)
XLA Modules:
  0.0 120.0 jit_solution(6585076711456213341)
XLA Ops:
  0.0 118.8 %influence.1 = f32[4,256]{1,0:T(4,128)} custom-call(bf16[4,256,1792]{2,1,0:T(8,128)(2,1)} %refs_0_.1, bf16[4,1792]{1,0:T(4,128)(2,1)} %bitcast.1, bf16[256,512]{1,0:T(8,128)(2,1)} %refs_2_.1, bf16[256,1792]{1,0:T(8,128)(2,1)} %refs_3_.1), custom_call_target="tpu_custom_call" | custom-call | flops 469762048 | bytes 5000000 | tf_op jit(solution)/shard_map/influence/pallas_call | solution.py:410
  118.8 1.3 %copy.6 = f32[4,256]{1,0:T(4,128)} copy(f32[4,256]{1,0:T(4,128)} %influence.1) | data formatting | bytes 8192

commit v2 on v1

--- a/solution.py
+++ b/solution.py
@@ -28,9 +28,11 @@
 
 TREE = {0: (1, -1), 3: (1, -1), -3: (1, -1), 6: (1, -1, 2), -6: (1, -1)}
 RELAYS = (6, -6, 3, -3)
-ARRIVALS = (3, -3, 6, -6)
+FAR = (8, 7, 9, 6, 10, 5, 11, 4, 12, 3, 13, 2, 14, 1, 15)
+FAN = {0: (1, -1, 2, -2), 5: (1, -1, 2, -2, 3), -5: (1, -1, 2, -2)}
 LEAVES = [(r, f) for r in (6, -6, 3, -3, 0) for f in TREE[r]]
-ORDER = (10, 6, 9, 7, 11, 5, 2, 14, 8, 13, 3, 15, 1, 12, 4)
+SIDE = 4
+ORDER = (10, 6, 14, 9, 11, 2, 8, 5, 15, 7, 13, 1, 3, 4, 12)
 
 
 def nt(a, b, precision=None):
@@ -88,7 +90,7 @@
         return lax.rem(z + offset + Z, Z)
 
     def peer(k):
-        return lax.rem(par + k, PAR)
+        return lax.rem(par // SIDE + k // SIDE, SIDE) * SIDE + lax.rem(par + k, SIDE)
 
     sent = []
     sibling = (tok + 1 - 2 * core, par)
@@ -100,17 +102,20 @@
         pltpu.make_async_copy(m.hook_out, m.ho, m.load_sem.at[QUERIES]),
         pltpu.make_async_copy(m.hook_in, m.hi, m.load_sem.at[QUERIES + 1]),
     ]
+    load_start = pltpu.make_async_copy(m.start, m.begin, m.load_sem.at[QUERIES + 2])
+    load_start.start()
     barrier = pltpu.get_barrier_semaphore()
-    for k in range(1, Z):
+    for k in FAR:
         pl.semaphore_signal(barrier, inc=1, device_id=chip(k), device_id_type=MESH)
     pl.semaphore_signal(barrier, inc=1, device_id=sibling, device_id_type=MESH)
-    for k in range(1, PAR):
+    for k in ORDER:
         pl.semaphore_signal(barrier, inc=1, device_id=(tok, peer(k)), device_id_type=MESH)
 
     for load in loads:
         load.start()
 
-    start = m.start[...].astype(F32)
+    load_start.wait()
+    start = m.begin[...].astype(F32)
     tail = jnp.concatenate(
         [start[:, 3 * PIECE :], jnp.zeros((start.shape[0], PIECES * PIECE - FEATS), F32)], axis=1
     )
@@ -124,14 +129,14 @@
 
     def z_gather(buf, send_sem, recv_sem):
         own = buf.at[z]
-        for r in RELAYS + TREE[0]:
+        for r in (5, -5) + FAN[0]:
             remote(own, own, send_sem, recv_sem.at[r % Z], chip(r)).start()
-        for r in ARRIVALS:
+        for r in (5, -5):
             block = buf.at[at_z(-r)]
             drain(block, recv_sem.at[r % Z])
-            for f in TREE[r]:
+            for f in FAN[r]:
                 remote(block, block, send_sem, recv_sem.at[(r + f) % Z], chip(f)).start()
-        relayed = [r % Z for r in RELAYS]
+        relayed = [r % Z for r in (5, -5)]
         for k in range(1, Z):
             if k not in relayed:
                 drain(buf.at[at_z(-k)], recv_sem.at[k])
@@ -182,7 +187,7 @@
         if it == ITERS - 1:
             @pl.when(z == par)
             def _():
-                for k in range(1, Z):
+                for k in FAR:
                     remote(
                         m.whole.at[it, at_z(k)], m.brow, m.brow_ss, m.brow_rs, chip(k)
                     ).start()
@@ -224,7 +229,7 @@
         drain(m.gram_in.at[it], m.gram_rs.at[it, 0])
         m.gram_rows[it] = (packed + m.gram_in[it]).reshape(PAR, 2, COLS)
         mine = m.gram_rows.at[it, par]
-        for k in range(1, Z):
+        for k in FAR:
             remote(
                 mine, m.gram_z.at[it, k - 1], m.gram_ss.at[it, 1], m.gram_rs.at[it, 1], chip(k)
             ).start()
@@ -351,7 +356,8 @@
         g=vmem((QUERIES, ROWS, FEATS), BF16),
         ho=vmem((ROWS, OUTS), BF16),
         hi=vmem((ROWS, FEATS), BF16),
-        load_sem=dma((QUERIES + 2,)),
+        begin=vmem((QUERIES, FEATS), BF16),
+        load_sem=dma((QUERIES + 3,)),
         s0=vmem((2, Z, 4 * PIECES, PIECE), BF16),
         s0_ss=dma((2,)),
         s0_rs=dma((Z,)),
@@ -411,7 +417,7 @@
         body,
         name="influence",
         out_shape=jax.ShapeDtypeStruct((QUERIES, ROWS), F32),
-        in_specs=[hbm, near, hbm, hbm],
+        in_specs=[hbm, hbm, hbm, hbm],
         out_specs=near,
         scratch_shapes=list(scratch.values()),
         compiler_params=pltpu.CompilerParams(

time: 120 us -> 118 us (0.983)
  Pallas kernels: 119 us -> 117 us
    pallas_call x1, Pallas kernels: 119 us -> 117 us  [on_device(): pl.pallas_call(body, name='influence', out_shape=jax.ShapeDtypeStruct((QU...]
where the time goes in v2:
time: 118 us
  Pallas kernels  117 us (99%)
  local copies, waits for them, and re-layouts  1.28 us (1%)
    pallas_call x1, Pallas kernels, on_device(): pl.pallas_call(body, name='influence', out_shape=jax.ShapeDtypeStruct((QU...  117 us

profile of v2, /device:TPU:1, one launch (start us, length us, event | category | flops | bytes accessed | tf_op | source)
XLA Modules:
  0.0 118.1 jit_solution(8036950021267209711)
XLA Ops:
  0.0 116.8 %influence.1 = f32[4,256]{1,0:T(4,128)} custom-call(bf16[4,256,1792]{2,1,0:T(8,128)(2,1)} %refs_0_.1, bf16[4,1792]{1,0:T(4,128)(2,1)} %bitcast.1, bf16[256,512]{1,0:T(8,128)(2,1)} %refs_2_.1, bf16[256,1792]{1,0:T(8,128)(2,1)} %refs_3_.1), custom_call_target="tpu_custom_call" | custom-call | flops 469762048 | bytes 5000000 | tf_op jit(solution)/shard_map/influence/pallas_call | solution.py:416
  116.8 1.3 %copy.6 = f32[4,256]{1,0:T(4,128)} copy(f32[4,256]{1,0:T(4,128)} %influence.1) | data formatting | bytes 8192

commit v3 on v2

--- a/solution.py
+++ b/solution.py
@@ -318,21 +318,24 @@
         [last[plane, :, HALF:, :].reshape(ROWS, COLS) for plane in range(2)], axis=0
     )
     out_proj = jnp.dot(m.ho[...], basis, preferred_element_type=F32)
+    m.proj[0] = out_proj.reshape(PAR, CHUNK, COLS)
+    par_scatter(m.proj.at[0], m.proj_in.at[0], m.proj_ss.at[0], m.proj_rs.at[0])
     subspace = jnp.concatenate(
         [tiles_of(last, q // 2, (q % 2) * RANK) for q in range(QUERIES)], axis=0
     )
     in_proj = nt(m.hi[...], subspace)
-    m.proj[:, :CHUNK, :] = out_proj.reshape(PAR, CHUNK, COLS)
-    m.proj[:, CHUNK:, :] = in_proj.reshape(PAR, CHUNK, COLS)
-    par_scatter(m.proj, m.proj_in, m.proj_ss, m.proj_rs)
+    m.proj[1] = in_proj.reshape(PAR, CHUNK, COLS)
+    par_scatter(m.proj.at[1], m.proj_in.at[1], m.proj_ss.at[1], m.proj_rs.at[1])
     lane8 = lax.broadcasted_iota(jnp.int32, (8, COLS), 1)
     row8 = lax.broadcasted_iota(jnp.int32, (8, COLS), 0)
     pick = jnp.where(lane8 // RANK == row8, 1.0, 0.0).astype(F32)
     m.placed[...] = jnp.zeros((LANES, COLS), F32)
-    drain(m.proj_in, m.proj_rs)
-    total = m.proj[par] + jnp.sum(m.proj_in[...], axis=0)
+    sums = []
+    for n in range(2):
+        drain(m.proj_in.at[n], m.proj_rs.at[n])
+        sums.append(m.proj[n, par] + jnp.sum(m.proj_in[n], axis=0))
     m.placed[pl.ds(pl.multiple_of((par % 8) * CHUNK, CHUNK), CHUNK), :] = (
-        total[:CHUNK] * total[CHUNK:]
+        sums[0] * sums[1]
     )
     m.score[par] = nt(pick, m.placed[...], HIGH)
     par_gather(m.score, m.score_ss, m.score_rs)
@@ -397,10 +400,10 @@
         last=vmem((2, Z, HALF + CHUNK, LANES), BF16),
         sub_ss=dma((ITERS, 2)),
         sub_rs=dma((ITERS, Z)),
-        proj=vmem((PAR, 2 * CHUNK, COLS), F32),
-        proj_in=vmem((PAR - 1, 2 * CHUNK, COLS), F32),
-        proj_ss=dma,
-        proj_rs=dma,
+        proj=vmem((2, PAR, CHUNK, COLS), F32),
+        proj_in=vmem((2, PAR - 1, CHUNK, COLS), F32),
+        proj_ss=dma((2,)),
+        proj_rs=dma((2,)),
         placed=vmem((LANES, COLS), F32),
         score=vmem((PAR, 8, LANES), F32),
         score_ss=dma,

time: 118 us -> 118 us (level)
  no operation moved by 1% of the time
where the time goes in v3:
time: 118 us
  Pallas kernels  117 us (99%)
  local copies, waits for them, and re-layouts  1.28 us (1%)
    pallas_call x1, Pallas kernels, on_device(): pl.pallas_call(body, name='influence', out_shape=jax.ShapeDtypeStruct((QU...  117 us

profile of v3, /device:TPU:1, one launch (start us, length us, event | category | flops | bytes accessed | tf_op | source)
XLA Modules:
  0.0 118.0 jit_solution(3620300285335760523)
XLA Ops:
  0.0 116.7 %influence.1 = f32[4,256]{1,0:T(4,128)} custom-call(bf16[4,256,1792]{2,1,0:T(8,128)(2,1)} %refs_0_.1, bf16[4,1792]{1,0:T(4,128)(2,1)} %bitcast.1, bf16[256,512]{1,0:T(8,128)(2,1)} %refs_2_.1, bf16[256,1792]{1,0:T(8,128)(2,1)} %refs_3_.1), custom_call_target="tpu_custom_call" | custom-call | flops 469762048 | bytes 5000000 | tf_op jit(solution)/shard_map/influence/pallas_call | solution.py:419
  116.7 1.3 %copy.6 = f32[4,256]{1,0:T(4,128)} copy(f32[4,256]{1,0:T(4,128)} %influence.1) | data formatting | bytes 8192
